TPU v7x, 512 devices: a whole 4x4x16 slice. The times are simulated.
512 devices in a mesh: grp: 32 (over z, core), pan: 16 (over y, x).
Axes of the slice: x: 4, y: 4, z: 16, core: 2. Of those that a mesh axis runs over, the one named last changes fastest.
Arguments:
- jblocks: bfloat16 [196608, 4096], P(('grp', 'pan')), may hold values from -240 to 240
- blk_row: int32 [196608], P(('grp', 'pan')), may hold values from 0 to 3
- blk_src: int32 [196608], P(('grp', 'pan')), may hold values from 0 to 31, as said below
- blk_slot: int32 [196608], P(('grp', 'pan')), may hold values from 0 to 7, as said below
- live_count: int32 [512], P(('grp', 'pan')), may hold values from 256 to 384, as said below
- send_list: int32 [32, 16, 32, 8], P('grp', 'pan'), may hold values from 0 to 31, as said below
- omega: bfloat16 [1048576, 128], P(('grp', 'pan')), may hold values from -6 to 6
Outputs:
- projected: bfloat16 [1048576, 128], P(('grp', 'pan'))
Inputs may be any that keep to these rules, and one draw needn't show every extreme that they name: `send_list`: within one row (owner, pan index, group) the 8 entries are distinct. On every device the first 256 stored blocks name each pair (blk_src, blk_slot) exactly once, in the order blk_src * 8 + blk_slot. `blk_slot`: see blk_src. `live_count`: some device has all 384 blocks live and some has only 256.
All inputs are finite; a program needn't handle non-finite values.
Results may differ from a plain program's by a relative error of at most 0.0012.
Values may be sent and summed in bfloat16 or wider, within the bound.
A program may use at most 128 MiB of HBM per device.

v0:
```python
import jax
import jax.numpy as jnp
from jax import lax
from jax.sharding import PartitionSpec as P

BLOCK = 64
RB_DEV = 4


def factor_of(sketch):
    local_gram = jnp.dot(sketch.T, sketch, precision=lax.Precision.HIGHEST)
    gram = lax.psum(local_gram, ("grp", "pan"))
    return jnp.linalg.cholesky(gram)


def per_device(jblocks, blk_row, blk_src, blk_slot, live_count, send_list, omega):
    block_count = jblocks.shape[0]
    width = omega.shape[1]
    groups = lax.axis_size("grp")
    lists = send_list.reshape(-1)
    slots = lists.shape[0]
    cap = slots // groups
    edge = BLOCK
    cell_blocks = omega.shape[0] // edge
    alive = jnp.arange(block_count, dtype=jnp.int32) < live_count[0]
    values = jnp.where(alive[:, None], jblocks, jnp.zeros((), jblocks.dtype)).reshape(
        block_count, edge, edge
    )
    omega_blocks = omega.reshape(cell_blocks, edge, width)
    outgoing = jnp.take(omega_blocks, lists, axis=0).reshape(groups, cap * edge, width)
    incoming = lax.all_to_all(outgoing, "grp", split_axis=0, concat_axis=0, tiled=True).reshape(
        slots, edge, width
    )
    slot_index = blk_src * cap + blk_slot
    picked = jnp.take(incoming, slot_index, axis=0)
    products = jnp.einsum("bij,bjk->bik", values, picked, preferred_element_type=jnp.float32)
    sketch = jax.ops.segment_sum(products, blk_row, num_segments=RB_DEV)
    sketch = sketch.reshape(RB_DEV * edge, width)
    lower = factor_of(sketch)
    used_rows = lax.linalg.triangular_solve(lower, sketch.T, left_side=True, lower=True).T
    chosen = jnp.take(used_rows.reshape(RB_DEV, edge, width), blk_row, axis=0)
    terms = jnp.einsum(
        "bij,bik->bjk",
        values.astype(jnp.float32),
        chosen,
        precision=lax.Precision.HIGH,
        preferred_element_type=jnp.float32,
    )
    per_slot = terms[:slots].at[slot_index[slots:]].add(terms[slots:])
    returned = lax.all_to_all(
        per_slot.reshape(groups, cap * edge, width), "grp", split_axis=0, concat_axis=0, tiled=True
    )
    empty = jnp.zeros((cell_blocks, edge, width), jnp.float32)
    summed = empty.at[lists].add(returned.reshape(slots, edge, width))
    summed = summed.reshape(cell_blocks * edge, width)
    return summed.astype(jnp.bfloat16)


def solution(mesh):
    placed = (
        P(("grp", "pan"), None),
        P(("grp", "pan")),
        P(("grp", "pan")),
        P(("grp", "pan")),
        P(("grp", "pan")),
        P("grp", "pan", None, None),
        P(("grp", "pan"), None),
    )
    return jax.shard_map(
        per_device, mesh=mesh, in_specs=placed, out_specs=P(("grp", "pan"), None), check_vma=False
    )
```

profile of v0, /device:TPU:1, one launch (start us, length us, event | category | flops | bytes accessed | tf_op | source)
XLA Modules:
  0.0 1202.4 jit_solution(17027515945941252848)
XLA Ops:
  6.5 0.0 copy-start
  6.5 0.8 copy.12
  7.4 0.7 compare_and_fusion
  8.1 0.1 reshape.89
  8.2 0.1 copy.14
  8.3 0.1 broadcast_in_dim.73
  8.4 0.1 broadcast_in_dim.74
  8.5 0.0 copy-done
  8.5 3.1 gather_fusion
  11.6 7.6 bitcast_select_fusion
  19.2 16.8 %all-to-all-start = ((bf16[32,512,128]{2,1,0:T(8,128)(2,1)}), bf16[32,512,128]{2,1,0:T(8,128)(2,1)}, u32[]{:S(2)}, u32[]{:S(2)}) async-start(bf16[32,512,128]{2,1,0:T(8,128)(2,1)} %bitcast_select_fusion), calls=%async_computation | async-start | bytes 8388608 | tf_op jit(solution)/shard_map/all_to_all | solution.py:31
  36.0 0.0 all-reduce.2.cloned.1.call-start
  36.0 4.7 copy.13
  41.4 3.9 broadcast_select_fusion
  45.2 0.0 copy-start.3
  45.2 0.0 copy-start.4
  45.3 0.0 copy-start.2
  45.3 12.3 %copy.18 = bf16[384,64,64]{1,2,0:T(8,128)(2,1)} copy(bf16[384,64,64]{0,2,1:T(8,128)(2,1)} %bitcast.39) | data formatting | bytes 6291456 | tf_op jit(solution)/shard_map/reshape | solution.py:26
  57.6 0.0 copy-done.3
  57.6 0.0 copy-done.4
  57.6 0.0 copy-done.2
  57.7 161.6 %all-to-all-done = bf16[32,512,128]{2,1,0:T(8,128)(2,1)} async-done(((bf16[32,512,128]{2,1,0:T(8,128)(2,1)}), bf16[32,512,128]{2,1,0:T(8,128)(2,1)}, u32[]{:S(2)}, u32[]{:S(2)}) %all-to-all-start) | async-done | bytes 4194336 | tf_op jit(solution)/shard_map/all_to_all | solution.py:31
  219.3 6.2 gather_fusion.1
  225.4 11.8 fusion.3
  237.2 40.0 %scatter_fusion = f32[4,64,128]{2,1,0:T(8,128)S(1)} fusion(f32[4,64,128]{2,1,0:T(8,128)S(1)} %broadcast_in_dim.70, s32[384]{0:T(512)S(1)} %copy-done.2, f32[384,64,128]{2,1,0:T(8,128)} %fusion.3), kind=kCustom, calls=%fused_computation.3 | custom fusion | flops 3145728 | bytes 37750272 | tf_op jit(solution)/shard_map/scatter-add | solution.py:37
  277.3 1.0 convolution_bitcast_fusion
  278.3 0.0 all-reduce.2.cloned.1.call-update
  278.3 439.3 %all-reduce.2.cloned.1.call-done = f32[128,128]{0,1:T(8,128)} async-done(((f32[128,128]{0,1:T(8,128)}), f32[128,128]{0,1:T(8,128)}) %all-reduce.2.cloned.1.call-update) | async-done | bytes 65552 | tf_op jit(solution)/shard_map/psum | solution.py:12
  717.6 0.9 copy.17
  718.5 0.9 fusion.11
  719.4 11.7 cholesky.16
  731.2 0.6 compare_reduce_fusion
  731.8 0.7 fusion.8
  732.5 9.8 custom-call.6
  742.3 0.3 fusion.9
  742.5 5.7 gather_fusion.2
  748.3 11.6 fusion
  759.8 8.2 slice.28
  768.1 4.7 slice.29
  772.8 20.2 %scatter_fusion.1 = f32[256,64,128]{2,1,0:T(8,128)} fusion(f32[256,64,128]{2,1,0:T(8,128)} %slice.28, s32[128]{0:T(128)S(1)} %compare_select_fusion.4, f32[128,64,128]{2,1,0:T(8,128)} %slice.29), kind=kCustom, calls=%fused_computation.4 | custom fusion | flops 1048576 | bytes 12583424 | tf_op jit(solution)/shard_map/scatter-add | solution.py:49
  793.0 375.4 %all_to_all.10 = f32[32,512,128]{2,1,0:T(8,128)} all-to-all(f32[32,512,128]{2,1,0:T(8,128)} %bitcast.36), channel_id=1, replica_groups=mesh['grp'=32,'pan'=16] {'grp'}, dimensions={0} | all-to-all | bytes 16777216 | tf_op jit(solution)/shard_map/all_to_all | solution.py:50
  1168.4 0.1 broadcast_in_dim.66
  1168.5 0.0 copy-start.1
  1168.5 26.1 %scatter_fusion.2 = f32[32,64,128]{2,1,0:T(8,128)S(1)} fusion(f32[32,64,128]{2,1,0:T(8,128)S(1)} %broadcast_in_dim.66, s32[256]{0:T(256)S(1)} %bitcast.41, f32[256,64,128]{2,1,0:T(8,128)} %bitcast.37), kind=kCustom, calls=%fused_computation.5 | custom fusion | flops 2097152 | bytes 25166848 | tf_op jit(solution)/shard_map/scatter-add | solution.py:54
  1194.7 0.9 convert_element_type.7
  1195.6 0.0 copy-done.1
  (12 shorter events, 0.1 us)
Async XLA Ops:
  6.5 1.9 copy-start
  19.2 200.1 %all-to-all-start = ((bf16[32,512,128]{2,1,0:T(8,128)(2,1)}), bf16[32,512,128]{2,1,0:T(8,128)(2,1)}, u32[]{:S(2)}, u32[]{:S(2)}) async-start(bf16[32,512,128]{2,1,0:T(8,128)(2,1)} %bitcast_select_fusion), calls=%async_computation | async-start | bytes 8388608 | tf_op jit(solution)/shard_map/all_to_all | solution.py:31
  36.0 681.6 %all-reduce.2.cloned.1.call-start = ((), (), s32[]{:S(2)}) async-start(), calls=%async_computation.2 | async-start | bytes 131072 | tf_op jit(solution)/shard_map/psum | solution.py:12
  45.2 12.3 %copy-start.3 = (s32[384]{0:T(512)S(1)}, s32[384]{0:T(512)}, u32[]{:S(2)}) copy-start(s32[384]{0:T(512)} %param.10) | copy-start | bytes 4612
  45.2 12.3 %copy-start.4 = (s32[384]{0:T(512)S(1)}, s32[384]{0:T(512)}, u32[]{:S(2)}) copy-start(s32[384]{0:T(512)} %param.9) | copy-start | bytes 4612
  45.3 12.4 %copy-start.2 = (s32[384]{0:T(512)S(1)}, s32[384]{0:T(512)}, u32[]{:S(2)}) copy-start(s32[384]{0:T(512)} %param.8) | copy-start | bytes 4612
  1168.5 27.0 %copy-start.1 = (bf16[2048,128]{1,0:T(8,128)(2,1)S(1)}, bf16[2048,128]{1,0:T(8,128)(2,1)}, u32[]{:S(2)}) copy-start(bf16[2048,128]{1,0:T(8,128)(2,1)} %param.13) | copy-start | bytes 1572868
Sparse Core Ops, SparseCore 0:
  278.4 439.1 all-reduce.1
where the time goes:
time: 1210 us; the launch traced here: 1200 us
  waiting for transfers between devices  601 us (50%)
  blocking collectives  375 us (31%)
  other arithmetic  123 us (10%)
  local copies, waits for them, and re-layouts  47.2 us (4%)
  matrix products  24.6 us (2%)
  starting transfers between devices  16.8 us (1%)
  between operations  14.2 us (1%)
    psum x1, waiting for transfers between devices, factor_of(): gram = lax.psum(local_gram, ('grp', 'pan'))  439 us
    all_to_all x1, blocking collectives, per_device(): lax.all_to_all(per_slot.reshape(groups, cap * edge, width), 'grp', split_...  375 us
    all_to_all x1, waiting for transfers between devices, per_device(): lax.all_to_all(outgoing, 'grp', split_axis=0, concat_axis=0, tiled=True)  162 us
    scatter-add x1, other arithmetic, per_device(): sketch = jax.ops.segment_sum(products, blk_row, num_segments=RB_DEV)  40 us
    scatter-add x1, other arithmetic, per_device(): summed = empty.at[lists].add(returned.reshape(slots, edge, width))  26.1 us
  transfers between devices with their start and end apart: 2, of which 2 were waited for; matrix products, arithmetic and copies ran while one was open for 2% of the time, Pallas kernels for 0%

commit v1 on v0

--- a/solution.py
+++ b/solution.py
@@ -1,10 +1,569 @@
+import functools
+
 import jax
 import jax.numpy as jnp
 from jax import lax
+from jax.experimental import pallas as pl
+from jax.experimental.pallas import tpu as pltpu
 from jax.sharding import PartitionSpec as P
 
 BLOCK = 64
 RB_DEV = 4
+PIECES = 2
+MOST_GAIN = 8.0
+MESH = pl.DeviceIdType.MESH
+HIGHEST = lax.Precision.HIGHEST
+
+
+def places(chips):
+    g = lax.axis_index("grp")
+    core = lax.rem(g, 2)
+    z = (g - core) // 2
+    up = lax.rem(z + 1, chips) * 2 + core
+    down = lax.rem(z + chips - 1, chips) * 2 + core
+    return g, core, z, up, down, g + 1 - 2 * core
+
+
+def greet(others):
+    barrier = pltpu.get_barrier_semaphore()
+    for other in others:
+        pl.semaphore_signal(barrier, inc=1, device_id={"grp": other}, device_id_type=MESH)
+    pl.semaphore_wait(barrier, len(others))
+
+
+def gather_kernel(
+    chips, mine, listed, gathered, lists, keep, ring_send, ring_recv, side_send, side_recv, own_send, own_recv,
+    list_send, list_recv, list_side_send, list_side_recv,
+):
+    g, core, z, up, down, side = places(chips)
+    half = chips // 2
+    step = mine.shape[0] // PIECES
+
+    def rows(piece):
+        return pl.ds(piece * step, step)
+
+    def owner(way, hop):
+        where = z + chips - hop if way == 0 else z + hop
+        return lax.rem(where, chips) * 2 + core
+
+    def ring(way, hop, piece, from_mine=False):
+        at = owner(way, hop - 1)
+        source = mine.at[rows(piece)] if from_mine else gathered.at[at, rows(piece)]
+        return pltpu.make_async_remote_copy(
+            src_ref=source,
+            dst_ref=gathered.at[at, rows(piece)],
+            send_sem=ring_send.at[way, hop - 1, piece],
+            recv_sem=ring_recv.at[way, hop - 1, piece],
+            device_id={"grp": up if way == 0 else down},
+            device_id_type=MESH,
+        )
+
+    def arrival(way, hop, piece):
+        at = owner(way, hop)
+        return pltpu.make_async_remote_copy(
+            src_ref=gathered.at[at, rows(piece)],
+            dst_ref=gathered.at[at, rows(piece)],
+            send_sem=ring_send.at[way, hop - 1, piece],
+            recv_sem=ring_recv.at[way, hop - 1, piece],
+            device_id={"grp": up if way == 0 else down},
+            device_id_type=MESH,
+        )
+
+    def across(way, hop, piece, arriving=False):
+        at = owner(way, hop) + (1 - 2 * core if arriving else 0)
+        return pltpu.make_async_remote_copy(
+            src_ref=gathered.at[at, rows(piece)],
+            dst_ref=gathered.at[at, rows(piece)],
+            send_sem=side_send.at[way, hop - 1, piece],
+            recv_sem=side_recv.at[way, hop - 1, piece],
+            device_id={"grp": side},
+            device_id_type=MESH,
+        )
+
+    def own(piece, at):
+        return pltpu.make_async_remote_copy(
+            src_ref=mine.at[rows(piece)],
+            dst_ref=gathered.at[at, rows(piece)],
+            send_sem=own_send.at[piece],
+            recv_sem=own_recv.at[piece],
+            device_id={"grp": side},
+            device_id_type=MESH,
+        )
+
+    def last(way):
+        return range(PIECES // 2) if way == 0 else range(PIECES // 2, PIECES)
+
+    def list_ring(way, hop):
+        at = owner(way, hop - 1)
+        return pltpu.make_async_remote_copy(
+            src_ref=lists.at[at],
+            dst_ref=lists.at[at],
+            send_sem=list_send.at[way, hop - 1],
+            recv_sem=list_recv.at[way, hop - 1],
+            device_id={"grp": up if way == 0 else down},
+            device_id_type=MESH,
+        )
+
+    def list_arrival(way, hop):
+        at = owner(way, hop)
+        return pltpu.make_async_remote_copy(
+            src_ref=lists.at[at],
+            dst_ref=lists.at[at],
+            send_sem=list_send.at[way, hop - 1],
+            recv_sem=list_recv.at[way, hop - 1],
+            device_id={"grp": up if way == 0 else down},
+            device_id_type=MESH,
+        )
+
+    def list_across(way, hop, arriving=False):
+        at = owner(way, hop) + (1 - 2 * core if arriving else 0)
+        return pltpu.make_async_remote_copy(
+            src_ref=lists.at[at],
+            dst_ref=lists.at[at],
+            send_sem=list_side_send.at[way, hop],
+            recv_sem=list_side_recv.at[way, hop],
+            device_id={"grp": side},
+            device_id_type=MESH,
+        )
+
+    greet((up, down, side))
+    kept = pltpu.make_async_copy(mine, gathered.at[g], keep.at[0])
+    kept.start()
+    listing = pltpu.make_async_copy(listed, lists.at[g], keep.at[1])
+    listing.start()
+    listing.wait()
+    list_ring(0, 1).start()
+    list_ring(1, 1).start()
+    list_across(0, 0).start()
+    for piece in range(PIECES):
+        for way in range(2):
+            ring(way, 1, piece, True).start()
+    for piece in range(PIECES):
+        own(piece, g).start()
+
+    def pass_on(hop, carry):
+        for way in range(2):
+            list_arrival(way, hop).wait_recv()
+            list_ring(way, hop + 1).start()
+            list_across(way, hop).start()
+        for piece in range(PIECES):
+            for way in range(2):
+                arrival(way, hop, piece).wait_recv()
+                ring(way, hop + 1, piece).start()
+                across(way, hop, piece).start()
+        return carry
+
+    lax.fori_loop(1, half - 1, pass_on, 0)
+    for way in range(2):
+        list_arrival(way, half - 1).wait_recv()
+        list_across(way, half - 1).start()
+    list_ring(0, half).start()
+    list_arrival(0, half).wait_recv()
+    list_across(0, half).start()
+    for piece in range(PIECES):
+        for way in range(2):
+            arrival(way, half - 1, piece).wait_recv()
+            if piece in last(way):
+                ring(way, half, piece).start()
+            across(way, half - 1, piece).start()
+    for way in range(2):
+        for piece in last(way):
+            arrival(way, half, piece).wait_recv()
+            across(way, half, piece).start()
+
+    for piece in range(PIECES):
+        ring(0, 1, piece, True).wait_send()
+        ring(1, 1, piece, True).wait_send()
+        own(piece, g).wait_send()
+        own(piece, side).wait_recv()
+
+    list_across(0, 0).wait_send()
+    list_across(0, 0, True).wait_recv()
+    list_ring(0, half).wait_send()
+    list_across(0, half).wait_send()
+    list_across(0, half, True).wait_recv()
+
+    def finish_lists(hop, carry):
+        for way in range(2):
+            list_ring(way, hop).wait_send()
+            list_across(way, hop).wait_send()
+            list_across(way, hop, True).wait_recv()
+        return carry
+
+    lax.fori_loop(1, half, finish_lists, 0)
+
+    def finish(hop, carry):
+        for piece in range(PIECES):
+            for way in range(2):
+                ring(way, hop + 1, piece).wait_send()
+                across(way, hop, piece).wait_send()
+                across(way, hop, piece, True).wait_recv()
+        return carry
+
+    lax.fori_loop(1, half - 1, finish, 0)
+    for piece in range(PIECES):
+        for way in range(2):
+            if piece in last(way):
+                ring(way, half, piece).wait_send()
+            across(way, half - 1, piece).wait_send()
+            across(way, half - 1, piece, True).wait_recv()
+    for way in range(2):
+        for piece in last(way):
+            across(way, half, piece).wait_send()
+            across(way, half, piece, True).wait_recv()
+    kept.wait()
+
+
+def gather(chips, omega, listed):
+    rows, width = omega.shape
+    half = chips // 2
+    dma = pltpu.SemaphoreType.DMA
+    hbm = pl.BlockSpec(memory_space=pl.ANY)
+    return pl.pallas_call(
+        functools.partial(gather_kernel, chips),
+        out_shape=[
+            jax.ShapeDtypeStruct((2 * chips, rows, width), omega.dtype),
+            jax.ShapeDtypeStruct((2 * chips,) + listed.shape, listed.dtype),
+        ],
+        in_specs=[hbm, hbm],
+        out_specs=[hbm, hbm],
+        scratch_shapes=[dma((2,))]
+        + [dma((2, half, PIECES))] * 4
+        + [dma((PIECES,))] * 2
+        + [dma((2, half))] * 2
+        + [dma((2, half + 1))] * 2,
+        compiler_params=pltpu.CompilerParams(collective_id=0, has_side_effects=True),
+    )(omega, listed)
+
+
+def local_kernel(
+    first, lists, blk_row, blk_src, blk_slot, live, x, cells, parts, gram, my_at, their_at, sketch, halves
+):
+    lane = lax.broadcasted_iota(jnp.int32, (1, 2 * BLOCK), 1)
+    blocks = x.shape[0]
+    owners, cap = lists.shape[0], lists.shape[1]
+    g = lax.axis_index("grp")
+    core = lax.rem(g, 2)
+    here = lax.broadcasted_iota(jnp.int32, (1, my_at.shape[1]), 1)
+
+    def row_of(at):
+        return jnp.where(at < live[0], blk_row[at], -1)
+
+    def slot_of(at):
+        return blk_src[at] * cap + blk_slot[at]
+
+    def place(owner, carry):
+        mine = jnp.full(here.shape, owners * cap, jnp.int32)
+        theirs = jnp.full(here.shape, owners // 2 * cap, jnp.int32)
+        for n in range(cap):
+            mine = jnp.where(here == lists[owner, n, g], owner * cap + n, mine)
+            theirs = jnp.where(here == lists[owner, n, g + 1 - 2 * core], owner // 2 * cap + n, theirs)
+        my_at[pl.ds(owner, 1), :] = mine
+        their_at[pl.ds(owner, 1), :] = theirs
+        return carry
+
+    lax.fori_loop(0, owners, place, 0)
+
+    def pair_of(at):
+        a, b = x[at], x[at + 1]
+        even = jnp.concatenate([a[:, :BLOCK], b[:, :BLOCK]], axis=1)
+        odd = jnp.concatenate([a[:, BLOCK:], b[:, BLOCK:]], axis=1)
+        both = jnp.concatenate([even, odd], axis=0)
+        rows = jnp.where(lane < BLOCK, row_of(at), row_of(at + 1))
+        return jnp.concatenate(
+            [both * jnp.where(rows == r, 1.0, 0.0).astype(both.dtype) for r in range(RB_DEV)], axis=0
+        )
+
+    def four_of(at):
+        return jnp.concatenate([pair_of(at), pair_of(at + 2)], axis=1)
+
+    def cell_rows(at):
+        first_row = lists[blk_src[at], blk_slot[at], g] * BLOCK
+        return cells[blk_src[at], pl.ds(pl.multiple_of(first_row, BLOCK), BLOCK), :]
+
+    sketch[...] = jnp.zeros_like(sketch)
+
+    def forward(i, carry):
+        at = i * 4
+        picked = jnp.concatenate([cell_rows(at + n) for n in range(4)], axis=0)
+        sketch[...] += jnp.dot(four_of(at), picked, preferred_element_type=jnp.float32)
+        return carry
+
+    lax.fori_loop(0, blocks // 4, forward, 0)
+    s = sketch[...]
+    gram[...] = lax.dot_general(
+        s, s, (((0,), (0,)), ((), ())), precision=HIGHEST, preferred_element_type=jnp.float32
+    )
+    high = s.astype(jnp.bfloat16)
+    low = (s - high.astype(jnp.float32)).astype(jnp.bfloat16)
+    halves[...] = jnp.concatenate([high, low], axis=1)
+    width = s.shape[1]
+
+    def back(at):
+        two = lax.dot_general(
+            four_of(at), halves[...], (((0,), (0,)), ((), ())), preferred_element_type=jnp.float32
+        )
+        return two[:, :width] + two[:, width:]
+
+    def base(i, carry):
+        out = back(i * 4)
+        for n in range(4):
+            parts[i * 4 + n] = out[n * BLOCK : (n + 1) * BLOCK]
+        return carry
+
+    lax.fori_loop(0, first // 4, base, 0)
+    parts[first] = jnp.zeros((BLOCK, width), jnp.float32)
+
+    def extra(i, carry):
+        out = back(i * 4)
+        for n in range(4):
+            parts[slot_of(i * 4 + n)] += out[n * BLOCK : (n + 1) * BLOCK]
+        return carry
+
+    lax.fori_loop(first // 4, blocks // 4, extra, 0)
+
+
+def local(first, lists, blk_row, blk_src, blk_slot, live, x, cells):
+    width = cells.shape[-1]
+    owners = cells.shape[0]
+    smem = pl.BlockSpec(memory_space=pltpu.SMEM)
+    vmem = pl.BlockSpec(memory_space=pltpu.VMEM)
+    return pl.pallas_call(
+        functools.partial(local_kernel, first),
+        out_shape=[
+            jax.ShapeDtypeStruct((first + 1, BLOCK, width), jnp.float32),
+            jax.ShapeDtypeStruct((width, width), jnp.float32),
+            jax.ShapeDtypeStruct((owners, width), jnp.int32),
+            jax.ShapeDtypeStruct((owners, width), jnp.int32),
+        ],
+        in_specs=[smem, smem, smem, smem, smem, vmem, vmem],
+        out_specs=[vmem] * 4,
+        scratch_shapes=[
+            pltpu.VMEM((RB_DEV * BLOCK, width), jnp.float32),
+            pltpu.VMEM((RB_DEV * BLOCK, 2 * width), jnp.bfloat16),
+        ],
+        compiler_params=pltpu.CompilerParams(vmem_limit_bytes=56 * 1024 * 1024),
+    )(lists, blk_row, blk_src, blk_slot, live, x, cells)
+
+
+def return_kernel(
+    chips, cap, parts, mine, theirs, out, other, sent, got, sent_scale, got_scale,
+    side_send, side_recv, ring_send, ring_recv, scale_send, scale_recv,
+):
+    g, core, z, up, down, side = places(chips)
+    half = chips // 2
+    count = out.shape[0]
+    size = count // PIECES
+    greet((up, down, side))
+
+    def chip(n):
+        return lax.rem(z + n, chips)
+
+    def across(n):
+        at = chip(n)
+        return pltpu.make_async_remote_copy(
+            src_ref=parts.at[pl.ds((at * 2 + 1 - core) * cap, cap)],
+            dst_ref=other.at[pl.ds(at * cap, cap)],
+            send_sem=side_send.at[n],
+            recv_sem=side_recv.at[n],
+            device_id={"grp": side},
+            device_id_type=MESH,
+        )
+
+    def blocks(piece):
+        return pl.ds(piece * size, size)
+
+    def ring(way, hop, piece):
+        to = {"grp": up if way == 0 else down}
+        values = pltpu.make_async_remote_copy(
+            src_ref=sent.at[way, hop, blocks(piece)],
+            dst_ref=got.at[way, hop, blocks(piece)],
+            send_sem=ring_send.at[way, hop, piece],
+            recv_sem=ring_recv.at[way, hop, piece],
+            device_id=to,
+            device_id_type=MESH,
+        )
+        scales = pltpu.make_async_remote_copy(
+            src_ref=sent_scale.at[way, hop, blocks(piece)],
+            dst_ref=got_scale.at[way, hop, blocks(piece)],
+            send_sem=scale_send.at[way, hop, piece],
+            recv_sem=scale_recv.at[way, hop, piece],
+            device_id=to,
+            device_id_type=MESH,
+        )
+        return values, scales
+
+    lax.fori_loop(0, chips, lambda n, c: (across(n).start(), c)[1], 0)
+    other[other.shape[0] - 1] = jnp.zeros(out.shape[1:], jnp.float32)
+    lax.fori_loop(0, chips, lambda n, c: (across(n).wait_recv(), c)[1], 0)
+
+    def own(target, q):
+        owner = target * 2 + core
+        return parts[mine[owner, q]] + other[theirs[owner, q]]
+
+    def read(way, hop, q):
+        return got[way, hop, q].astype(jnp.int32).astype(jnp.float32) * got_scale[way, hop, pl.ds(q, 1), :]
+
+    def await_piece(way, hop, piece):
+        for copy in ring(way, hop, piece):
+            copy.wait_recv()
+
+    def send(way, hop, piece, onward):
+        target = chip(half - hop if way == 0 else chips - half + hop)
+        if onward:
+            await_piece(way, hop - 1, piece)
+
+        def block(q, carry):
+            total = own(target, q)
+            if onward:
+                total = total + read(way, hop - 1, q)
+            top = jnp.max(jnp.abs(total), axis=0, keepdims=True)
+            usable = top > 1e-30
+            factor = jnp.where(usable, 32767.0 / jnp.where(usable, top, 1.0), 0.0)
+            sent[way, hop, q] = jnp.round(total * factor).astype(jnp.int32).astype(jnp.int16)
+            sent_scale[way, hop, pl.ds(q, 1), :] = top * (1.0 / 32767.0)
+            return carry
+
+        lax.fori_loop(piece * size, (piece + 1) * size, block, 0)
+        for copy in ring(way, hop, piece):
+            copy.start()
+
+    def first(way):
+        return range(PIECES // 2) if way == 0 else range(PIECES // 2, PIECES)
+
+    for way in range(2):
+        for piece in first(way):
+            send(way, 0, piece, False)
+    for piece in range(PIECES):
+        for way in range(2):
+            send(way, 1, piece, piece in first(way))
+
+    def onward(hop, carry):
+        for piece in range(PIECES):
+            for way in range(2):
+                send(way, hop, piece, True)
+        return carry
+
+    lax.fori_loop(2, half, onward, 0)
+    for piece in range(PIECES):
+        for way in range(2):
+            await_piece(way, half - 1, piece)
+
+        def block(q, carry):
+            out[q] = own(z, q) + read(0, half - 1, q) + read(1, half - 1, q)
+            return carry
+
+        lax.fori_loop(piece * size, (piece + 1) * size, block, 0)
+
+    def finish(way, hop, piece):
+        for copy in ring(way, hop, piece):
+            copy.wait_send()
+
+    for way in range(2):
+        for piece in first(way):
+            finish(way, 0, piece)
+
+    def finish_all(hop, carry):
+        for piece in range(PIECES):
+            for way in range(2):
+                finish(way, hop, piece)
+        return carry
+
+    lax.fori_loop(1, half, finish_all, 0)
+    lax.fori_loop(0, chips, lambda n, c: (across(n).wait_send(), c)[1], 0)
+
+
+def give_back(chips, cap, count, parts, mine, theirs):
+    edge, width = parts.shape[1:]
+    half = chips // 2
+    dma = pltpu.SemaphoreType.DMA
+    smem = pl.BlockSpec(memory_space=pltpu.SMEM)
+    vmem = pl.BlockSpec(memory_space=pltpu.VMEM)
+    return pl.pallas_call(
+        functools.partial(return_kernel, chips, cap),
+        out_shape=jax.ShapeDtypeStruct((count, edge, width), jnp.float32),
+        in_specs=[vmem, smem, smem],
+        out_specs=vmem,
+        scratch_shapes=[
+            pltpu.VMEM((chips * cap + 1, edge, width), jnp.float32),
+            pltpu.VMEM((2, half, count, edge, width), jnp.int16),
+            pltpu.VMEM((2, half, count, edge, width), jnp.int16),
+            pltpu.VMEM((2, half, count, width), jnp.float32),
+            pltpu.VMEM((2, half, count, width), jnp.float32),
+            dma((chips,)),
+            dma((chips,)),
+            dma((2, half, PIECES)),
+            dma((2, half, PIECES)),
+            dma((2, half, PIECES)),
+            dma((2, half, PIECES)),
+        ],
+        compiler_params=pltpu.CompilerParams(
+            collective_id=1, has_side_effects=True, vmem_limit_bytes=56 * 1024 * 1024
+        ),
+    )(parts, mine, theirs)
+
+
+def finish_kernel(gram, z, out, gain, a, v):
+    n = gram.shape[0]
+    lane = lax.broadcasted_iota(jnp.int32, (n, n), 1)
+    sub = lax.broadcasted_iota(jnp.int32, (n, n), 0)
+    a[...] = gram[...]
+    v[...] = jnp.where(lane == sub, 1.0, 0.0)
+
+    def pivot(j, carry):
+        old = a[...]
+        row_a, row_v = a[pl.ds(j, 1), :], v[pl.ds(j, 1), :]
+        d = jnp.sum(jnp.where(lane[:1] == j, row_a, 0.0), axis=1, keepdims=True)
+        column = jnp.sum(jnp.where(lane == j, old, 0.0), axis=1, keepdims=True)
+        factor = jnp.where(sub > j, column / d, 0.0)
+        a[...] = old - factor * row_a
+        v[...] = v[...] - factor * row_v
+        return carry
+
+    lax.fori_loop(0, n, pivot, 0)
+    d = jnp.sum(jnp.where(lane == sub, a[...], 0.0), axis=1, keepdims=True)
+    inverse = v[...] / jnp.sqrt(d)
+    spread = jnp.sum(jnp.where(lane == sub, gram[...], 0.0), axis=0, keepdims=True)
+    grown = jnp.sum(inverse * inverse * spread, axis=1, keepdims=True)
+    gain[...] = jnp.broadcast_to(jnp.sum(grown, axis=0, keepdims=True), gain.shape)
+    high = inverse.astype(jnp.bfloat16)
+    low = (inverse - high.astype(jnp.float32)).astype(jnp.bfloat16)
+    factors = jnp.concatenate(
+        [
+            jnp.concatenate([high, high], axis=1),
+            jnp.concatenate([low, jnp.zeros_like(low)], axis=1),
+        ],
+        axis=0,
+    )
+
+    def rows(i, carry):
+        at = pl.ds(pl.multiple_of(i * 256, 256), 256)
+        value = z[at, :]
+        top = value.astype(jnp.bfloat16)
+        rest = (value - top.astype(jnp.float32)).astype(jnp.bfloat16)
+        two = lax.dot_general(
+            jnp.concatenate([top, rest], axis=1), factors, (((1,), (1,)), ((), ())),
+            preferred_element_type=jnp.float32,
+        )
+        out[at, :] = (two[:, :n] + two[:, n:]).astype(out.dtype)
+        return carry
+
+    lax.fori_loop(0, z.shape[0] // 256, rows, 0)
+
+
+def finish(gram, z):
+    n = gram.shape[0]
+    vmem = pl.BlockSpec(memory_space=pltpu.VMEM)
+    return pl.pallas_call(
+        finish_kernel,
+        out_shape=[
+            jax.ShapeDtypeStruct(z.shape, jnp.bfloat16),
+            jax.ShapeDtypeStruct((8, n), jnp.float32),
+        ],
+        in_specs=[vmem, vmem],
+        out_specs=[vmem, vmem],
+        scratch_shapes=[pltpu.VMEM((n, n), jnp.float32), pltpu.VMEM((n, n), jnp.float32)],
+    )(gram, z)
 
 
 def factor_of(sketch):
@@ -13,7 +572,7 @@
     return jnp.linalg.cholesky(gram)
 
 
-def per_device(jblocks, blk_row, blk_src, blk_slot, live_count, send_list, omega):
+def careful(jblocks, blk_row, blk_src, blk_slot, live_count, send_list, omega):
     block_count = jblocks.shape[0]
     width = omega.shape[1]
     groups = lax.axis_size("grp")
@@ -56,6 +615,27 @@
     return summed.astype(jnp.bfloat16)
 
 
+def per_device(jblocks, blk_row, blk_src, blk_slot, live_count, send_list, omega):
+    blocks = jblocks.shape[0]
+    chips, cap = lax.axis_size("grp") // 2, send_list.shape[-1]
+    width = omega.shape[1]
+    first = 2 * chips * cap
+    count = omega.shape[0] // BLOCK
+    listed = jnp.pad(send_list[0, 0].T, ((0, 0), (0, width - 2 * chips)))
+    gathered, lists = gather(chips, omega, listed)
+    x = jblocks.reshape(blocks, BLOCK // 2, 2 * BLOCK)
+    parts, gram, my_at, their_at = local(first, lists, blk_row, blk_src, blk_slot, live_count, x, gathered)
+    total = lax.psum(gram, ("grp", "pan"))
+    z = give_back(chips, cap, count, parts, my_at, their_at)
+    projected, gain = finish(total, z.reshape(count * BLOCK, width))
+    return lax.cond(
+        gain[0, 0] <= MOST_GAIN * width,
+        lambda *given: projected,
+        careful,
+        jblocks, blk_row, blk_src, blk_slot, live_count, send_list, omega,
+    )
+
+
 def solution(mesh):
     placed = (
         P(("grp", "pan"), None),

time: 1210 us -> 649 us (0.54)
  blocking collectives: 375 us -> 0 us
  Pallas kernels: 0 us -> 292 us
  waiting for transfers between devices: 601 us -> 335 us
  other arithmetic: 123 us -> 0 us
  local copies, waits for them, and re-layouts: 47.2 us -> 6.43 us
  matrix products: 24.6 us -> 0 us
  starting transfers between devices: 16.8 us -> 0.04 us
    all_to_all x1 -> x0, blocking collectives: 375 us -> none  [per_device(): lax.all_to_all(per_slot.reshape(groups, cap * edge, width), 'grp', split_...]
    pallas_call x0 -> x4, Pallas kernels: none -> 292 us  [the longest x1 108 us: give_back(): pl.pallas_call(functools.partial(return_kernel, chips, cap), out_shape=ja...]
    all_to_all x1 -> x0, waiting for transfers between devices: 162 us -> none  [per_device(): lax.all_to_all(outgoing, 'grp', split_axis=0, concat_axis=0, tiled=True)]
    psum x1, waiting for transfers between devices: 439 us -> 335 us  [per_device(): total = lax.psum(gram, ('grp', 'pan'))]
    scatter-add x3 -> x0, other arithmetic: 86.4 us -> none  [the longest x1 40 us: per_device(): sketch = jax.ops.segment_sum(products, blk_row, num_segments=RB_DEV)]
    dot_general x3 -> x0, matrix products: 24.4 us -> none  [the longest x1 11.8 us: per_device(): jnp.einsum('bij,bjk->bik', values, picked, preferred_element_type=jnp.flo...]
    another operation x5 -> x0, other arithmetic: 22.9 us -> none  [the longest x3 12.4 us: factor_of(): return jnp.linalg.cholesky(gram)]
    all_to_all x1 -> x0, starting transfers between devices: 16.8 us -> none  [per_device(): lax.all_to_all(outgoing, 'grp', split_axis=0, concat_axis=0, tiled=True)]
  transfers between devices with their start and end apart: 2 -> 1, of which waited for: 2 -> 1; matrix products, arithmetic and copies ran while one was open for 2% -> 0% of each run, Pallas kernels for 0% -> 17%
where the time goes in v1:
time: 649 us; the launch traced here: 648 us
  waiting for transfers between devices  335 us (52%)
  Pallas kernels  292 us (45%)
  between operations  14.8 us (2%)
    psum x1, waiting for transfers between devices, per_device(): total = lax.psum(gram, ('grp', 'pan'))  335 us
    pallas_call x1, Pallas kernels, give_back(): pl.pallas_call(functools.partial(return_kernel, chips, cap), out_shape=ja...  108 us
    pallas_call x1, Pallas kernels, gather(): pl.pallas_call(functools.partial(gather_kernel, chips), out_shape=[jax.Sh...  104 us
    pallas_call x1, Pallas kernels, local(): pl.pallas_call(functools.partial(local_kernel, first), out_shape=[jax.Sha...  62.1 us
    pallas_call x1, Pallas kernels, finish(): pl.pallas_call(finish_kernel, out_shape=[jax.ShapeDtypeStruct(z.shape, jn...  17.4 us
  transfers between devices with their start and end apart: 1, of which 1 were waited for; matrix products, arithmetic and copies ran while one was open for 0% of the time, Pallas kernels for 17%

profile of v1, /device:TPU:1, one launch (start us, length us, event | category | flops | bytes accessed | tf_op | source)
XLA Modules:
  0.0 648.3 jit_solution(16719631749204431579)
XLA Ops:
  6.5 0.0 copy-start.3
  6.5 0.0 copy-start
  6.5 0.0 copy-start.2
  6.5 0.0 copy-start.4
  6.5 0.0 copy-start.5
  6.5 0.0 all-reduce.6.cloned.1.call-start
  6.6 4.5 copy.22
  11.8 0.0 copy-done.3
  11.8 0.6 pad.4.listed
  12.4 0.0 copy-done
  12.4 104.3 %shard_map.75 = (bf16[32,2048,128]{2,1,0:T(8,128)(2,1)}, s32[32,8,128]{2,1,0:T(8,128)}) custom-call(bf16[2048,128]{1,0:T(8,128)(2,1)S(1)} %copy-done, s32[8,128]{1,0:T(8,128)} %pad.4.listed), custom_call_target="tpu_custom_call" | custom-call | tf_op jit(solution)/shard_map/pallas_call | solution.py:222
  116.7 0.0 copy-done.2
  116.8 0.0 copy-done.4
  116.8 0.0 copy-done.5
  116.8 62.1 %shard_map.76 = (f32[257,64,128]{2,1,0:T(8,128)}, f32[128,128]{1,0:T(8,128)}, s32[32,128]{1,0:T(8,128)}, s32[32,128]{1,0:T(8,128)}) custom-call(s32[32,8,128]{2,1,0:T(8,128)} %get-tuple-element.38.lists, s32[384]{0:T(512)S(1)} %copy-done.2, s32[384]{0:T(512)S(1)} %copy-done.4, s32[384]{0:T(512)S(1)} %copy-done.5, s32[1]{0:T(128)S(6)} %copy.30.live, ...), custom_call_target="tpu_custom_call" | custom-call | tf_op jit(solution)/shard_map/pallas_call | solution.py:331
  178.8 0.0 all-reduce.6.cloned.1.call-update
  178.9 108.3 %shard_map.77 = f32[32,64,128]{2,1,0:T(8,128)} custom-call(f32[257,64,128]{2,1,0:T(8,128)} %get-tuple-element.41.parts, s32[32,128]{1,0:T(8,128)} %get-tuple-element.42.mine, s32[32,128]{1,0:T(8,128)} %get-tuple-element.43.theirs), custom_call_target="tpu_custom_call" | custom-call | tf_op jit(solution)/shard_map/pallas_call | solution.py:482
  287.2 334.7 %all-reduce.6.cloned.1.call-done.gram = f32[128,128]{1,0:T(8,128)} async-done(((f32[128,128]{1,0:T(8,128)}), f32[128,128]{1,0:T(8,128)}) %all-reduce.6.cloned.1.call-update) | async-done | bytes 65552 | tf_op jit(solution)/shard_map/psum | solution.py:628
  621.9 17.4 %shard_map.78 = (bf16[2048,128]{1,0:T(8,128)(2,1)}, f32[8,128]{1,0:T(8,128)}) custom-call(f32[128,128]{1,0:T(8,128)} %all-reduce.6.cloned.1.call-done.gram, f32[2048,128]{1,0:T(8,128)} %bitcast.48), custom_call_target="tpu_custom_call" | custom-call | tf_op jit(solution)/shard_map/pallas_call | solution.py:557
  639.3 1.3 slice.22
  641.2 0.2 conditional.1
Async XLA Ops:
  6.5 5.3 copy-start.3
  6.5 5.9 copy-start
  6.5 110.2 %copy-start.2 = (s32[384]{0:T(512)S(1)}, s32[384]{0:T(512)}, u32[]{:S(2)}) copy-start(s32[384]{0:T(512)} %blk_row.1) | copy-start | bytes 4612
  6.5 110.2 %copy-start.4 = (s32[384]{0:T(512)S(1)}, s32[384]{0:T(512)}, u32[]{:S(2)}) copy-start(s32[384]{0:T(512)} %blk_src.1) | copy-start | bytes 4612
  6.5 110.2 %copy-start.5 = (s32[384]{0:T(512)S(1)}, s32[384]{0:T(512)}, u32[]{:S(2)}) copy-start(s32[384]{0:T(512)} %blk_slot.1) | copy-start | bytes 4612
  6.5 615.4 %all-reduce.6.cloned.1.call-start = ((), (), s32[]{:S(2)}) async-start(), calls=%async_computation.3 | async-start | bytes 131072 | tf_op jit(solution)/shard_map/psum | solution.py:628
Sparse Core Ops, SparseCore 0:
  179.0 442.8 all-reduce.5

commit v2 on v1

--- a/solution.py
+++ b/solution.py
@@ -10,6 +10,7 @@
 BLOCK = 64
 RB_DEV = 4
 PIECES = 2
+SOME = 8
 MOST_GAIN = 8.0
 MESH = pl.DeviceIdType.MESH
 HIGHEST = lax.Precision.HIGHEST
@@ -254,10 +255,10 @@
 
     def place(owner, carry):
         mine = jnp.full(here.shape, owners * cap, jnp.int32)
-        theirs = jnp.full(here.shape, owners // 2 * cap, jnp.int32)
+        theirs = jnp.full(here.shape, cap, jnp.int32)
         for n in range(cap):
             mine = jnp.where(here == lists[owner, n, g], owner * cap + n, mine)
-            theirs = jnp.where(here == lists[owner, n, g + 1 - 2 * core], owner // 2 * cap + n, theirs)
+            theirs = jnp.where(here == lists[owner, n, g + 1 - 2 * core], n, theirs)
         my_at[pl.ds(owner, 1), :] = mine
         their_at[pl.ds(owner, 1), :] = theirs
         return carry
@@ -274,8 +275,8 @@
             [both * jnp.where(rows == r, 1.0, 0.0).astype(both.dtype) for r in range(RB_DEV)], axis=0
         )
 
-    def four_of(at):
-        return jnp.concatenate([pair_of(at), pair_of(at + 2)], axis=1)
+    def some_of(at):
+        return jnp.concatenate([pair_of(at + n) for n in range(0, SOME, 2)], axis=1)
 
     def cell_rows(at):
         first_row = lists[blk_src[at], blk_slot[at], g] * BLOCK
@@ -284,12 +285,12 @@
     sketch[...] = jnp.zeros_like(sketch)
 
     def forward(i, carry):
-        at = i * 4
-        picked = jnp.concatenate([cell_rows(at + n) for n in range(4)], axis=0)
-        sketch[...] += jnp.dot(four_of(at), picked, preferred_element_type=jnp.float32)
-        return carry
-
-    lax.fori_loop(0, blocks // 4, forward, 0)
+        at = i * SOME
+        picked = jnp.concatenate([cell_rows(at + n) for n in range(SOME)], axis=0)
+        sketch[...] += jnp.dot(some_of(at), picked, preferred_element_type=jnp.float32)
+        return carry
+
+    lax.fori_loop(0, blocks // SOME, forward, 0, unroll=2)
     s = sketch[...]
     gram[...] = lax.dot_general(
         s, s, (((0,), (0,)), ((), ())), precision=HIGHEST, preferred_element_type=jnp.float32
@@ -301,26 +302,26 @@
 
     def back(at):
         two = lax.dot_general(
-            four_of(at), halves[...], (((0,), (0,)), ((), ())), preferred_element_type=jnp.float32
+            some_of(at), halves[...], (((0,), (0,)), ((), ())), preferred_element_type=jnp.float32
         )
         return two[:, :width] + two[:, width:]
 
     def base(i, carry):
-        out = back(i * 4)
-        for n in range(4):
-            parts[i * 4 + n] = out[n * BLOCK : (n + 1) * BLOCK]
-        return carry
-
-    lax.fori_loop(0, first // 4, base, 0)
+        made = back(i * SOME)
+        for n in range(SOME):
+            parts[i * SOME + n] = made[n * BLOCK : (n + 1) * BLOCK]
+        return carry
+
+    lax.fori_loop(0, first // SOME, base, 0, unroll=2)
     parts[first] = jnp.zeros((BLOCK, width), jnp.float32)
 
     def extra(i, carry):
-        out = back(i * 4)
-        for n in range(4):
-            parts[slot_of(i * 4 + n)] += out[n * BLOCK : (n + 1) * BLOCK]
-        return carry
-
-    lax.fori_loop(first // 4, blocks // 4, extra, 0)
+        made = back(i * SOME)
+        for n in range(SOME):
+            parts[slot_of(i * SOME + n)] += made[n * BLOCK : (n + 1) * BLOCK]
+        return carry
+
+    lax.fori_loop(first // SOME, blocks // SOME, extra, 0)
 
 
 def local(first, lists, blk_row, blk_src, blk_slot, live, x, cells):
@@ -346,29 +347,100 @@
     )(lists, blk_row, blk_src, blk_slot, live, x, cells)
 
 
+def flip(index, step):
+    return index + step - 2 * step * lax.rem(index // step, 2)
+
+
+def sum_kernel(axis, rounds, value, total, held, got, send, recv):
+    at = lax.axis_index(axis)
+    barrier = pltpu.get_barrier_semaphore()
+    for i in range(rounds):
+        pl.semaphore_signal(barrier, inc=1, device_id={axis: flip(at, 1 << i)}, device_id_type=MESH)
+    pl.semaphore_wait(barrier, rounds)
+    held[0] = value[...]
+    copies = []
+    for i in range(rounds):
+        copy = pltpu.make_async_remote_copy(
+            src_ref=held.at[i], dst_ref=got.at[i], send_sem=send.at[i], recv_sem=recv.at[i],
+            device_id={axis: flip(at, 1 << i)}, device_id_type=MESH,
+        )
+        copy.start()
+        copy.wait_recv()
+        held[i + 1] = held[i] + got[i]
+        copies.append(copy)
+    total[...] = held[rounds]
+    for copy in copies:
+        copy.wait_send()
+
+
+def sum_over(axis, size, value):
+    rounds = size.bit_length() - 1
+    if rounds == 0:
+        return value
+    vmem = pl.BlockSpec(memory_space=pltpu.VMEM)
+    return pl.pallas_call(
+        functools.partial(sum_kernel, axis, rounds),
+        out_shape=jax.ShapeDtypeStruct(value.shape, value.dtype),
+        in_specs=[vmem],
+        out_specs=vmem,
+        scratch_shapes=[
+            pltpu.VMEM((rounds + 1,) + value.shape, value.dtype),
+            pltpu.VMEM((rounds,) + value.shape, value.dtype),
+            pltpu.SemaphoreType.DMA((rounds,)),
+            pltpu.SemaphoreType.DMA((rounds,)),
+        ],
+        compiler_params=pltpu.CompilerParams(collective_id=2, has_side_effects=True),
+    )(value)
+
+
 def return_kernel(
-    chips, cap, parts, mine, theirs, out, other, sent, got, sent_scale, got_scale,
-    side_send, side_recv, ring_send, ring_recv, scale_send, scale_recv,
+    chips, cap, rounds, parts, gram, mine, theirs, out, gain,
+    other_far, other_next, other, sent, got, sent_scale, got_scale, grams, grams_got, a, v, factors, z_buf,
+    side_send, side_recv, ring_send, ring_recv, scale_send, scale_recv, gram_send, gram_recv,
 ):
     g, core, z, up, down, side = places(chips)
     half = chips // 2
-    count = out.shape[0]
+    width = out.shape[1]
+    count = out.shape[0] // BLOCK
     size = count // PIECES
-    greet((up, down, side))
+    met = [flip(g, 1 << i) for i in range(rounds)]
+    greet([up, down, side] + met)
+
+    def gram_copy(i):
+        return pltpu.make_async_remote_copy(
+            src_ref=grams.at[i], dst_ref=grams_got.at[i], send_sem=gram_send.at[i], recv_sem=gram_recv.at[i],
+            device_id={"grp": met[i]}, device_id_type=MESH,
+        )
+
+    def gram_round(i):
+        gram_copy(i).wait_recv()
+        grams[i + 1] = grams[i] + grams_got[i]
+        if i + 1 < rounds:
+            gram_copy(i + 1).start()
 
     def chip(n):
         return lax.rem(z + n, chips)
 
-    def across(n):
+    def across(n, to):
         at = chip(n)
         return pltpu.make_async_remote_copy(
             src_ref=parts.at[pl.ds((at * 2 + 1 - core) * cap, cap)],
-            dst_ref=other.at[pl.ds(at * cap, cap)],
+            dst_ref=to.at[pl.ds(0, cap)],
             send_sem=side_send.at[n],
             recv_sem=side_recv.at[n],
             device_id={"grp": side},
             device_id_type=MESH,
         )
+
+    early = [(half, other_far.at[0]), (half - 1, other_next.at[0]), (half + 1, other_next.at[1])]
+
+    def rest(act):
+        def one(n, carry):
+            act(across(n, other.at[n]))
+            return carry
+
+        lax.fori_loop(0, half - 1, one, 0)
+        lax.fori_loop(half + 2, chips, one, 0)
 
     def blocks(piece):
         return pl.ds(piece * size, size)
@@ -393,13 +465,23 @@
         )
         return values, scales
 
-    lax.fori_loop(0, chips, lambda n, c: (across(n).start(), c)[1], 0)
-    other[other.shape[0] - 1] = jnp.zeros(out.shape[1:], jnp.float32)
-    lax.fori_loop(0, chips, lambda n, c: (across(n).wait_recv(), c)[1], 0)
-
-    def own(target, q):
-        owner = target * 2 + core
-        return parts[mine[owner, q]] + other[theirs[owner, q]]
+    for n, to in early:
+        across(n, to).start()
+    rest(lambda copy: copy.start())
+    grams[0] = gram[...]
+    gram_copy(0).start()
+    nothing = jnp.zeros((BLOCK, width), jnp.float32)
+    other_far[0, cap] = nothing
+    for n in range(2):
+        other_next[n, cap] = nothing
+    for n in range(chips):
+        other[n, cap] = nothing
+
+    def own(n, q, held=None, line=0):
+        owner = chip(n) * 2 + core
+        if held is None:
+            return parts[mine[owner, q]] + other[n, theirs[owner, q]]
+        return parts[mine[owner, q]] + held[line, theirs[owner, q]]
 
     def read(way, hop, q):
         return got[way, hop, q].astype(jnp.int32).astype(jnp.float32) * got_scale[way, hop, pl.ds(q, 1), :]
@@ -408,13 +490,13 @@
         for copy in ring(way, hop, piece):
             copy.wait_recv()
 
-    def send(way, hop, piece, onward):
-        target = chip(half - hop if way == 0 else chips - half + hop)
+    def send(way, hop, piece, onward, held=None):
+        n = half - hop if way == 0 else half + hop
         if onward:
             await_piece(way, hop - 1, piece)
 
         def block(q, carry):
-            total = own(target, q)
+            total = own(n, q, held, way if held is other_next else 0)
             if onward:
                 total = total + read(way, hop - 1, q)
             top = jnp.max(jnp.abs(total), axis=0, keepdims=True)
@@ -431,29 +513,96 @@
     def first(way):
         return range(PIECES // 2) if way == 0 else range(PIECES // 2, PIECES)
 
+    wide = lax.broadcasted_iota(jnp.int32, (width, width), 1)
+    tall = lax.broadcasted_iota(jnp.int32, (width, width), 0)
+
+    def pivot(j, carry):
+        old = a[...]
+        row_a, row_v = a[pl.ds(j, 1), :], v[pl.ds(j, 1), :]
+        d = jnp.sum(jnp.where(wide[:1] == j, row_a, 0.0), axis=1, keepdims=True)
+        column = jnp.sum(jnp.where(wide == j, old, 0.0), axis=1, keepdims=True)
+        factor = jnp.where(tall > j, column / d, 0.0)
+        a[...] = old - factor * row_a
+        v[...] = v[...] - factor * row_v
+        return carry
+
+    across(*early[0]).wait_recv()
     for way in range(2):
         for piece in first(way):
-            send(way, 0, piece, False)
+            send(way, 0, piece, False, other_far)
+    gram_round(0)
+    for n, to in early[1:]:
+        across(n, to).wait_recv()
+    turn = 1
     for piece in range(PIECES):
         for way in range(2):
-            send(way, 1, piece, piece in first(way))
+            at = PIECES - 1 - piece if way == 0 else piece
+            send(way, 1, at, at in first(way), other_next)
+            if turn < rounds:
+                gram_round(turn)
+                turn += 1
+    while turn < rounds:
+        gram_round(turn)
+        turn += 1
+    a[...] = grams[rounds]
+    v[...] = jnp.where(wide == tall, 1.0, 0.0)
+    rest(lambda copy: copy.wait_recv())
+    points = (half - 2) * PIECES * 2
+    each = width // points
+    lead = width - each * points
+    lax.fori_loop(0, lead, pivot, 0)
 
     def onward(hop, carry):
         for piece in range(PIECES):
             for way in range(2):
-                send(way, hop, piece, True)
+                send(way, hop, PIECES - 1 - piece if way == 0 else piece, True)
+                start = lead + (((hop - 2) * PIECES + piece) * 2 + way) * each
+                lax.fori_loop(start, start + each, pivot, 0)
         return carry
 
     lax.fori_loop(2, half, onward, 0)
+
+    d = jnp.sum(jnp.where(wide == tall, a[...], 0.0), axis=1, keepdims=True)
+    inverse = v[...] / jnp.sqrt(d)
+    spread = jnp.sum(jnp.where(wide == tall, grams[rounds], 0.0), axis=0, keepdims=True)
+    grown = jnp.sum(inverse * inverse * spread, axis=1, keepdims=True)
+    gain[...] = jnp.broadcast_to(jnp.sum(grown, axis=0, keepdims=True), gain.shape)
+    high = inverse.astype(jnp.bfloat16)
+    low = (inverse - high.astype(jnp.float32)).astype(jnp.bfloat16)
+    factors[...] = jnp.concatenate(
+        [
+            jnp.concatenate([high, high], axis=1),
+            jnp.concatenate([low, jnp.zeros_like(low)], axis=1),
+        ],
+        axis=0,
+    )
+
     for piece in range(PIECES):
         for way in range(2):
             await_piece(way, half - 1, piece)
 
         def block(q, carry):
-            out[q] = own(z, q) + read(0, half - 1, q) + read(1, half - 1, q)
+            z_buf[pl.ds(pl.multiple_of(q * BLOCK, BLOCK), BLOCK), :] = (
+                own(0, q) + read(0, half - 1, q) + read(1, half - 1, q)
+            )
             return carry
 
         lax.fori_loop(piece * size, (piece + 1) * size, block, 0)
+
+        def product(i, carry):
+            at = pl.ds(pl.multiple_of(i * 256, 256), 256)
+            value = z_buf[at, :]
+            top = value.astype(jnp.bfloat16)
+            left = (value - top.astype(jnp.float32)).astype(jnp.bfloat16)
+            two = lax.dot_general(
+                jnp.concatenate([top, left], axis=1), factors[...], (((1,), (1,)), ((), ())),
+                preferred_element_type=jnp.float32,
+            )
+            out[at, :] = (two[:, :width] + two[:, width:]).astype(out.dtype)
+            return carry
+
+        per = size * BLOCK // 256
+        lax.fori_loop(piece * per, (piece + 1) * per, product, 0)
 
     def finish(way, hop, piece):
         for copy in ring(way, hop, piece):
@@ -470,100 +619,56 @@
         return carry
 
     lax.fori_loop(1, half, finish_all, 0)
-    lax.fori_loop(0, chips, lambda n, c: (across(n).wait_send(), c)[1], 0)
-
-
-def give_back(chips, cap, count, parts, mine, theirs):
+    for n, to in early:
+        across(n, to).wait_send()
+    rest(lambda copy: copy.wait_send())
+    for i in range(rounds):
+        gram_copy(i).wait_send()
+
+
+def give_back(chips, cap, count, parts, gram, mine, theirs):
     edge, width = parts.shape[1:]
     half = chips // 2
+    rounds = (2 * chips).bit_length() - 1
     dma = pltpu.SemaphoreType.DMA
     smem = pl.BlockSpec(memory_space=pltpu.SMEM)
     vmem = pl.BlockSpec(memory_space=pltpu.VMEM)
+    f32 = jnp.float32
     return pl.pallas_call(
-        functools.partial(return_kernel, chips, cap),
-        out_shape=jax.ShapeDtypeStruct((count, edge, width), jnp.float32),
-        in_specs=[vmem, smem, smem],
-        out_specs=vmem,
+        functools.partial(return_kernel, chips, cap, rounds),
+        out_shape=[
+            jax.ShapeDtypeStruct((count * edge, width), jnp.bfloat16),
+            jax.ShapeDtypeStruct((8, width), f32),
+        ],
+        in_specs=[vmem, vmem, smem, smem],
+        out_specs=[vmem, vmem],
         scratch_shapes=[
-            pltpu.VMEM((chips * cap + 1, edge, width), jnp.float32),
+            pltpu.VMEM((1, cap + 1, edge, width), f32),
+            pltpu.VMEM((2, cap + 1, edge, width), f32),
+            pltpu.VMEM((chips, cap + 1, edge, width), f32),
             pltpu.VMEM((2, half, count, edge, width), jnp.int16),
             pltpu.VMEM((2, half, count, edge, width), jnp.int16),
-            pltpu.VMEM((2, half, count, width), jnp.float32),
-            pltpu.VMEM((2, half, count, width), jnp.float32),
+            pltpu.VMEM((2, half, count, width), f32),
+            pltpu.VMEM((2, half, count, width), f32),
+            pltpu.VMEM((rounds + 1, width, width), f32),
+            pltpu.VMEM((rounds, width, width), f32),
+            pltpu.VMEM((width, width), f32),
+            pltpu.VMEM((width, width), f32),
+            pltpu.VMEM((2 * width, 2 * width), jnp.bfloat16),
+            pltpu.VMEM((count * edge, width), f32),
             dma((chips,)),
             dma((chips,)),
             dma((2, half, PIECES)),
             dma((2, half, PIECES)),
             dma((2, half, PIECES)),
             dma((2, half, PIECES)),
+            dma((rounds,)),
+            dma((rounds,)),
         ],
         compiler_params=pltpu.CompilerParams(
             collective_id=1, has_side_effects=True, vmem_limit_bytes=56 * 1024 * 1024
         ),
-    )(parts, mine, theirs)
-
-
-def finish_kernel(gram, z, out, gain, a, v):
-    n = gram.shape[0]
-    lane = lax.broadcasted_iota(jnp.int32, (n, n), 1)
-    sub = lax.broadcasted_iota(jnp.int32, (n, n), 0)
-    a[...] = gram[...]
-    v[...] = jnp.where(lane == sub, 1.0, 0.0)
-
-    def pivot(j, carry):
-        old = a[...]
-        row_a, row_v = a[pl.ds(j, 1), :], v[pl.ds(j, 1), :]
-        d = jnp.sum(jnp.where(lane[:1] == j, row_a, 0.0), axis=1, keepdims=True)
-        column = jnp.sum(jnp.where(lane == j, old, 0.0), axis=1, keepdims=True)
-        factor = jnp.where(sub > j, column / d, 0.0)
-        a[...] = old - factor * row_a
-        v[...] = v[...] - factor * row_v
-        return carry
-
-    lax.fori_loop(0, n, pivot, 0)
-    d = jnp.sum(jnp.where(lane == sub, a[...], 0.0), axis=1, keepdims=True)
-    inverse = v[...] / jnp.sqrt(d)
-    spread = jnp.sum(jnp.where(lane == sub, gram[...], 0.0), axis=0, keepdims=True)
-    grown = jnp.sum(inverse * inverse * spread, axis=1, keepdims=True)
-    gain[...] = jnp.broadcast_to(jnp.sum(grown, axis=0, keepdims=True), gain.shape)
-    high = inverse.astype(jnp.bfloat16)
-    low = (inverse - high.astype(jnp.float32)).astype(jnp.bfloat16)
-    factors = jnp.concatenate(
-        [
-            jnp.concatenate([high, high], axis=1),
-            jnp.concatenate([low, jnp.zeros_like(low)], axis=1),
-        ],
-        axis=0,
-    )
-
-    def rows(i, carry):
-        at = pl.ds(pl.multiple_of(i * 256, 256), 256)
-        value = z[at, :]
-        top = value.astype(jnp.bfloat16)
-        rest = (value - top.astype(jnp.float32)).astype(jnp.bfloat16)
-        two = lax.dot_general(
-            jnp.concatenate([top, rest], axis=1), factors, (((1,), (1,)), ((), ())),
-            preferred_element_type=jnp.float32,
-        )
-        out[at, :] = (two[:, :n] + two[:, n:]).astype(out.dtype)
-        return carry
-
-    lax.fori_loop(0, z.shape[0] // 256, rows, 0)
-
-
-def finish(gram, z):
-    n = gram.shape[0]
-    vmem = pl.BlockSpec(memory_space=pltpu.VMEM)
-    return pl.pallas_call(
-        finish_kernel,
-        out_shape=[
-            jax.ShapeDtypeStruct(z.shape, jnp.bfloat16),
-            jax.ShapeDtypeStruct((8, n), jnp.float32),
-        ],
-        in_specs=[vmem, vmem],
-        out_specs=[vmem, vmem],
-        scratch_shapes=[pltpu.VMEM((n, n), jnp.float32), pltpu.VMEM((n, n), jnp.float32)],
-    )(gram, z)
+    )(parts, gram, mine, theirs)
 
 
 def factor_of(sketch):
@@ -625,9 +730,8 @@
     gathered, lists = gather(chips, omega, listed)
     x = jblocks.reshape(blocks, BLOCK // 2, 2 * BLOCK)
     parts, gram, my_at, their_at = local(first, lists, blk_row, blk_src, blk_slot, live_count, x, gathered)
-    total = lax.psum(gram, ("grp", "pan"))
-    z = give_back(chips, cap, count, parts, my_at, their_at)
-    projected, gain = finish(total, z.reshape(count * BLOCK, width))
+    gram = sum_over("pan", lax.axis_size("pan"), gram)
+    projected, gain = give_back(chips, cap, count, parts, gram, my_at, their_at)
     return lax.cond(
         gain[0, 0] <= MOST_GAIN * width,
         lambda *given: projected,

time: 649 us -> 323 us (0.50)
  waiting for transfers between devices: 335 us -> 0 us
  Pallas kernels: 292 us -> 299 us
    psum x1 -> x0, waiting for transfers between devices: 335 us -> none  [per_device(): total = lax.psum(gram, ('grp', 'pan'))]
    pallas_call x1, Pallas kernels: 62.1 us -> 32.8 us  [local(): pl.pallas_call(functools.partial(local_kernel, first), out_shape=[jax.Sha...]
    pallas_call x2, Pallas kernels: 126 us -> 146 us  [the longest x1 128 us: give_back(): pl.pallas_call(functools.partial(return_kernel, chips, cap, rounds), out_...]
    pallas_call x1, Pallas kernels: 104 us -> 120 us  [gather(): pl.pallas_call(functools.partial(gather_kernel, chips), out_shape=[jax.Sh...]
  transfers between devices with their start and end apart: 1 -> 0, of which waited for: 1 -> 0; matrix products, arithmetic and copies ran while one was open for 0% -> 0% of each run, Pallas kernels for 17% -> 0%
where the time goes in v2:
time: 323 us
  Pallas kernels  299 us (93%)
  between operations  14.8 us (5%)
  local copies, waits for them, and re-layouts  8.89 us (3%)
    pallas_call x1, Pallas kernels, give_back(): pl.pallas_call(functools.partial(return_kernel, chips, cap, rounds), out_...  128 us
    pallas_call x1, Pallas kernels, gather(): pl.pallas_call(functools.partial(gather_kernel, chips), out_shape=[jax.Sh...  120 us
    pallas_call x1, Pallas kernels, local(): pl.pallas_call(functools.partial(local_kernel, first), out_shape=[jax.Sha...  32.8 us
    pallas_call x1, Pallas kernels, sum_over(): pl.pallas_call(functools.partial(sum_kernel, axis, rounds), out_shape=jax...  18.2 us

profile of v2, /device:TPU:1, one launch (start us, length us, event | category | flops | bytes accessed | tf_op | source)
XLA Modules:
  0.0 322.7 jit_solution(761121324432608161)
XLA Ops:
  6.5 0.0 copy-start.2
  6.5 0.0 copy-start.4
  6.5 0.0 copy-start.5
  6.5 1.3 pad.4.listed
  7.9 120.2 %shard_map.75 = (bf16[32,2048,128]{2,1,0:T(8,128)(2,1)}, s32[32,8,128]{2,1,0:T(8,128)}) custom-call(bf16[2048,128]{1,0:T(8,128)(2,1)} %mine.1, s32[8,128]{1,0:T(8,128)} %pad.4.listed), custom_call_target="tpu_custom_call" | custom-call | tf_op jit(solution)/shard_map/pallas_call | solution.py:223
  128.1 4.5 %copy.22 = bf16[48,8,32,128]{3,2,1,0:T(8,128)(2,1)} copy(bf16[48,8,32,128]{3,1,2,0:T(8,128)(2,1)} %bitcast.45) | data formatting | bytes 6291456
  133.2 0.0 copy-done.2
  133.2 0.0 copy-done.4
  133.3 0.0 copy-done.5
  133.3 32.8 %shard_map.76 = (f32[257,64,128]{2,1,0:T(8,128)}, f32[128,128]{1,0:T(8,128)}, s32[32,128]{1,0:T(8,128)}, s32[32,128]{1,0:T(8,128)}) custom-call(s32[32,8,128]{2,1,0:T(8,128)} %get-tuple-element.38.lists, s32[384]{0:T(512)S(1)} %copy-done.2, s32[384]{0:T(512)S(1)} %copy-done.4, s32[384]{0:T(512)S(1)} %copy-done.5, s32[1]{0:T(128)S(6)} %copy.30.live, ...), custom_call_target="tpu_custom_call" | custom-call | tf_op jit(solution)/shard_map/pallas_call | solution.py:332
  166.1 0.0 copy-start
  166.1 0.0 copy-start.3
  166.1 18.2 %shard_map.77.gram = f32[128,128]{1,0:T(8,128)} custom-call(f32[128,128]{1,0:T(8,128)} %get-tuple-element.41.value), custom_call_target="tpu_custom_call" | custom-call | tf_op jit(solution)/shard_map/pallas_call | solution.py:381
  184.3 127.6 %shard_map.78 = (bf16[2048,128]{1,0:T(8,128)(2,1)}, f32[8,128]{1,0:T(8,128)}) custom-call(f32[257,64,128]{2,1,0:T(8,128)} %get-tuple-element.40.parts, f32[128,128]{1,0:T(8,128)} %shard_map.77.gram, s32[32,128]{1,0:T(8,128)} %get-tuple-element.42.mine, s32[32,128]{1,0:T(8,128)} %get-tuple-element.43.theirs), custom_call_target="tpu_custom_call" | custom-call | tf_op jit(solution)/shard_map/pallas_call | solution.py:637
  311.9 1.2 slice.22
  313.8 0.0 copy-done
  313.8 0.0 copy-done.3
  313.8 0.2 conditional.1
  314.0 1.9 copy.31
Async XLA Ops:
  6.5 126.7 %copy-start.2 = (s32[384]{0:T(512)S(1)}, s32[384]{0:T(512)}, u32[]{:S(2)}) copy-start(s32[384]{0:T(512)} %blk_row.1) | copy-start | bytes 4612
  6.5 126.7 %copy-start.4 = (s32[384]{0:T(512)S(1)}, s32[384]{0:T(512)}, u32[]{:S(2)}) copy-start(s32[384]{0:T(512)} %blk_src.1) | copy-start | bytes 4612
  6.5 126.7 %copy-start.5 = (s32[384]{0:T(512)S(1)}, s32[384]{0:T(512)}, u32[]{:S(2)}) copy-start(s32[384]{0:T(512)} %blk_slot.1) | copy-start | bytes 4612
  166.1 147.7 %copy-start = (bf16[2048,128]{1,0:T(8,128)(2,1)S(1)}, bf16[2048,128]{1,0:T(8,128)(2,1)}, u32[]{:S(2)}) copy-start(bf16[2048,128]{1,0:T(8,128)(2,1)} %mine.1) | copy-start | bytes 1572868
  166.1 147.7 %copy-start.3 = (s32[1,1,32,8]{2,3,1,0:T(8,128)S(1)}, s32[1,1,32,8]{2,3,1,0:T(8,128)}, u32[]{:S(2)}) copy-start(s32[1,1,32,8]{2,3,1,0:T(8,128)} %param.14) | copy-start | bytes 3076

commit v3 on v2

--- a/solution.py
+++ b/solution.py
@@ -11,6 +11,7 @@
 RB_DEV = 4
 PIECES = 2
 SOME = 8
+GROUP = 4
 MOST_GAIN = 8.0
 MESH = pl.DeviceIdType.MESH
 HIGHEST = lax.Precision.HIGHEST
@@ -495,18 +496,23 @@
         if onward:
             await_piece(way, hop - 1, piece)
 
-        def block(q, carry):
-            total = own(n, q, held, way if held is other_next else 0)
-            if onward:
-                total = total + read(way, hop - 1, q)
-            top = jnp.max(jnp.abs(total), axis=0, keepdims=True)
-            usable = top > 1e-30
-            factor = jnp.where(usable, 32767.0 / jnp.where(usable, top, 1.0), 0.0)
-            sent[way, hop, q] = jnp.round(total * factor).astype(jnp.int32).astype(jnp.int16)
-            sent_scale[way, hop, pl.ds(q, 1), :] = top * (1.0 / 32767.0)
+        def some(i, carry):
+            made = []
+            for q in [i * GROUP + k for k in range(GROUP)]:
+                total = own(n, q, held, way if held is other_next else 0)
+                if onward:
+                    total = total + read(way, hop - 1, q)
+                top = jnp.max(jnp.abs(total), axis=0, keepdims=True)
+                usable = top > 1e-30
+                factor = jnp.where(usable, 32767.0 / jnp.where(usable, top, 1.0), 0.0)
+                value = jnp.round(total * factor).astype(jnp.int32).astype(jnp.int16)
+                made.append((q, value, top * (1.0 / 32767.0)))
+            for q, value, scale in made:
+                sent[way, hop, q] = value
+                sent_scale[way, hop, pl.ds(q, 1), :] = scale
             return carry
 
-        lax.fori_loop(piece * size, (piece + 1) * size, block, 0)
+        lax.fori_loop(piece * size // GROUP, (piece + 1) * size // GROUP, some, 0)
         for copy in ring(way, hop, piece):
             copy.start()
 
@@ -581,13 +587,15 @@
         for way in range(2):
             await_piece(way, half - 1, piece)
 
-        def block(q, carry):
-            z_buf[pl.ds(pl.multiple_of(q * BLOCK, BLOCK), BLOCK), :] = (
-                own(0, q) + read(0, half - 1, q) + read(1, half - 1, q)
-            )
+        def some(i, carry):
+            made = []
+            for q in [i * GROUP + k for k in range(GROUP)]:
+                made.append((q, own(0, q) + read(0, half - 1, q) + read(1, half - 1, q)))
+            for q, value in made:
+                z_buf[pl.ds(pl.multiple_of(q * BLOCK, BLOCK), BLOCK), :] = value
             return carry
 
-        lax.fori_loop(piece * size, (piece + 1) * size, block, 0)
+        lax.fori_loop(piece * size // GROUP, (piece + 1) * size // GROUP, some, 0)
 
         def product(i, carry):
             at = pl.ds(pl.multiple_of(i * 256, 256), 256)

time: 323 us -> 322 us (level)
  no operation moved by 1% of the time
where the time goes in v3:
time: 322 us
  Pallas kernels  298 us (93%)
  between operations  14.8 us (5%)
  local copies, waits for them, and re-layouts  8.89 us (3%)
    pallas_call x1, Pallas kernels, give_back(): pl.pallas_call(functools.partial(return_kernel, chips, cap, rounds), out_...  127 us
    pallas_call x1, Pallas kernels, gather(): pl.pallas_call(functools.partial(gather_kernel, chips), out_shape=[jax.Sh...  120 us
    pallas_call x1, Pallas kernels, local(): pl.pallas_call(functools.partial(local_kernel, first), out_shape=[jax.Sha...  32.8 us
    pallas_call x1, Pallas kernels, sum_over(): pl.pallas_call(functools.partial(sum_kernel, axis, rounds), out_shape=jax...  18.2 us

profile of v3, /device:TPU:1, one launch (start us, length us, event | category | flops | bytes accessed | tf_op | source)
XLA Modules:
  0.0 322.0 jit_solution(353802370711424399)
XLA Ops:
  6.5 0.0 copy-start.2
  6.5 0.0 copy-start.4
  6.5 0.0 copy-start.5
  6.5 1.3 pad.4.listed
  7.9 120.2 %shard_map.75 = (bf16[32,2048,128]{2,1,0:T(8,128)(2,1)}, s32[32,8,128]{2,1,0:T(8,128)}) custom-call(bf16[2048,128]{1,0:T(8,128)(2,1)} %mine.1, s32[8,128]{1,0:T(8,128)} %pad.4.listed), custom_call_target="tpu_custom_call" | custom-call | tf_op jit(solution)/shard_map/pallas_call | solution.py:224
  128.1 4.5 %copy.22 = bf16[48,8,32,128]{3,2,1,0:T(8,128)(2,1)} copy(bf16[48,8,32,128]{3,1,2,0:T(8,128)(2,1)} %bitcast.45) | data formatting | bytes 6291456
  133.2 0.0 copy-done.2
  133.2 0.0 copy-done.4
  133.3 0.0 copy-done.5
  133.3 32.8 %shard_map.76 = (f32[257,64,128]{2,1,0:T(8,128)}, f32[128,128]{1,0:T(8,128)}, s32[32,128]{1,0:T(8,128)}, s32[32,128]{1,0:T(8,128)}) custom-call(s32[32,8,128]{2,1,0:T(8,128)} %get-tuple-element.38.lists, s32[384]{0:T(512)S(1)} %copy-done.2, s32[384]{0:T(512)S(1)} %copy-done.4, s32[384]{0:T(512)S(1)} %copy-done.5, s32[1]{0:T(128)S(6)} %copy.30.live, ...), custom_call_target="tpu_custom_call" | custom-call | tf_op jit(solution)/shard_map/pallas_call | solution.py:333
  166.1 0.0 copy-start
  166.1 0.0 copy-start.3
  166.1 18.2 %shard_map.77.gram = f32[128,128]{1,0:T(8,128)} custom-call(f32[128,128]{1,0:T(8,128)} %get-tuple-element.41.value), custom_call_target="tpu_custom_call" | custom-call | tf_op jit(solution)/shard_map/pallas_call | solution.py:382
  184.3 126.9 %shard_map.78 = (bf16[2048,128]{1,0:T(8,128)(2,1)}, f32[8,128]{1,0:T(8,128)}) custom-call(f32[257,64,128]{2,1,0:T(8,128)} %get-tuple-element.40.parts, f32[128,128]{1,0:T(8,128)} %shard_map.77.gram, s32[32,128]{1,0:T(8,128)} %get-tuple-element.42.mine, s32[32,128]{1,0:T(8,128)} %get-tuple-element.43.theirs), custom_call_target="tpu_custom_call" | custom-call | tf_op jit(solution)/shard_map/pallas_call | solution.py:645
  311.2 1.2 slice.22
  313.0 0.0 copy-done
  313.0 0.0 copy-done.3
  313.0 0.2 conditional.1
  313.3 1.9 copy.31
Async XLA Ops:
  6.5 126.7 %copy-start.2 = (s32[384]{0:T(512)S(1)}, s32[384]{0:T(512)}, u32[]{:S(2)}) copy-start(s32[384]{0:T(512)} %blk_row.1) | copy-start | bytes 4612
  6.5 126.7 %copy-start.4 = (s32[384]{0:T(512)S(1)}, s32[384]{0:T(512)}, u32[]{:S(2)}) copy-start(s32[384]{0:T(512)} %blk_src.1) | copy-start | bytes 4612
  6.5 126.7 %copy-start.5 = (s32[384]{0:T(512)S(1)}, s32[384]{0:T(512)}, u32[]{:S(2)}) copy-start(s32[384]{0:T(512)} %blk_slot.1) | copy-start | bytes 4612
  166.1 146.9 %copy-start = (bf16[2048,128]{1,0:T(8,128)(2,1)S(1)}, bf16[2048,128]{1,0:T(8,128)(2,1)}, u32[]{:S(2)}) copy-start(bf16[2048,128]{1,0:T(8,128)(2,1)} %mine.1) | copy-start | bytes 1572868
  166.1 146.9 %copy-start.3 = (s32[1,1,32,8]{2,3,1,0:T(8,128)S(1)}, s32[1,1,32,8]{2,3,1,0:T(8,128)}, u32[]{:S(2)}) copy-start(s32[1,1,32,8]{2,3,1,0:T(8,128)} %param.14) | copy-start | bytes 3076
